TPU v7x, 32 devices: a whole 2x2x4 slice. The times are simulated.
32 devices in a mesh: row: 4 (over z), col: 8 (over y, x, core).
Axes of the slice: x: 2, y: 2, z: 4, core: 2. Of those that a mesh axis runs over, the one named last changes fastest.
Arguments:
- inputs: bfloat16 [4096, 2048], P('row', 'col'), may hold values from -6 to 6
- query_weight: bfloat16 [2048, 2048], P('row', 'col'), may hold values from -0.125 to 0.125
- key_weight: bfloat16 [2048, 2048], P('row', 'col'), may hold values from -0.125 to 0.125
- value_weight: bfloat16 [2048, 2048], P('row', 'col'), may hold values from -0.125 to 0.125
- out_weight: bfloat16 [2048, 2048], P('row', 'col'), may hold values from -2 to 2
- gate_weight: bfloat16 [2048, 8192], P('row', 'col'), may hold values from -0.125 to 0.125
- up_weight: bfloat16 [2048, 8192], P('row', 'col'), may hold values from -0.125 to 0.125
- down_weight: bfloat16 [2048, 8192], P('row', 'col'), may hold values from -0.0625 to 0.0625
- first_gain: bfloat16 [2048], P('row'), may hold values from 0.5 to 1.5
- second_gain: bfloat16 [2048], P('row'), may hold values from 0.5 to 1.5
- segment_ids: int32 [4096], P('row'), may hold values from 0 to 7, as said below
- positions: int32 [4096], P('row'), may hold values from 0 to 767, as said below
- out_grad: bfloat16 [4096, 2048], P('row', 'col'), may hold values from -6 to 6
Outputs:
- block_out: bfloat16 [4096, 2048], P('row', 'col')
- input_grad: bfloat16 [4096, 2048], P('row', 'col')
- query_weight_grad: float32 [2048, 2048], P('row', 'col')
- key_weight_grad: float32 [2048, 2048], P('row', 'col')
- value_weight_grad: float32 [2048, 2048], P('row', 'col')
- out_weight_grad: float32 [2048, 2048], P('row', 'col')
- gate_weight_grad: float32 [2048, 8192], P('row', 'col')
- up_weight_grad: float32 [2048, 8192], P('row', 'col')
- down_weight_grad: float32 [2048, 8192], P('row', 'col')
- first_gain_grad: float32 [2048], P('row')
- second_gain_grad: float32 [2048], P('row')
Inputs may be any that keep to these rules, and one draw needn't show every extreme that they name: `segment_ids`: ids never fall along the rows. Each aligned block of 1024 rows holds two documents, numbered 2 b and 2 b + 1 in block b; the second starts at a row from 256 to 768 of its block. `positions`: each row's offset from the first row of its document.
All inputs are finite; a program needn't handle non-finite values.
Results may differ from a plain program's by a relative error of at most 0.019.
Values may be sent and summed in bfloat16 or wider, within the bound.
No kernel may reach another device: no remote copies, remote signals or barrier semaphores. Data moves between devices by JAX's collectives and lax.ppermute only.
A program may use at most 192 MiB of HBM per device.

v0:
```python
import math
import jax
import jax.numpy as jnp
from jax import lax
from jax.sharding import PartitionSpec as P

HEAD_DIM = 64
SEQ = 1024
eps = 1e-05
rope_base = 130000.0


def rope_tables(positions, head_size):
    half_size = head_size // 2
    freqs = jnp.exp(
        jnp.arange(half_size, dtype=jnp.float32) * (-2.0 * math.log(rope_base) / head_size)
    )
    angles = positions.astype(jnp.float32)[:, None] * freqs[None, :]
    return (jnp.cos(angles), jnp.sin(angles))


def rotate(values, cosine, sine):
    half_size = values.shape[-1] // 2
    front_half = values[..., :half_size]
    back_half = values[..., half_size:]
    cosine_wide = cosine[:, None, :]
    sine_wide = sine[:, None, :]
    return jnp.concatenate(
        [
            front_half * cosine_wide - back_half * sine_wide,
            back_half * cosine_wide + front_half * sine_wide,
        ],
        axis=-1,
    )


def unrotate(values, cosine, sine):
    half_size = values.shape[-1] // 2
    front_half = values[..., :half_size]
    back_half = values[..., half_size:]
    cosine_wide = cosine[:, None, :]
    sine_wide = sine[:, None, :]
    return jnp.concatenate(
        [
            front_half * cosine_wide + back_half * sine_wide,
            back_half * cosine_wide - front_half * sine_wide,
        ],
        axis=-1,
    )


def contract_last(left, right):
    return lax.dot_general(
        left, right, (((1,), (1,)), ((), ())), preferred_element_type=jnp.float32
    )


def contract_first(left, right):
    return lax.dot_general(
        left, right, (((0,), (0,)), ((), ())), preferred_element_type=jnp.float32
    )


def block_mask(segment_ids, row_start, seq_start, block_rows):
    query_ids = lax.dynamic_slice_in_dim(segment_ids, row_start, block_rows, 0)
    query_index = row_start + jnp.arange(block_rows)
    key_index = seq_start + jnp.arange(SEQ)
    return (query_ids[:, None] == segment_ids[None, :]) & (
        query_index[:, None] >= key_index[None, :]
    )


def block_scores(query_piece, key_piece, allowed):
    scores = jnp.einsum(
        "qhd,khd->hqk", query_piece, key_piece, preferred_element_type=jnp.float32
    ) * HEAD_DIM ** (-0.5)
    return jnp.where(allowed[None], scores, -1e30)


def attend_forward(query_rows, key_rows, value_rows, segment_ids):
    token_count, heads_here, head_size = query_rows.shape
    block_rows = min(512, SEQ)
    block_count = token_count // block_rows

    def one_block(index_block):
        row_start = index_block * block_rows
        seq_start = row_start // SEQ * SEQ
        query_piece = lax.dynamic_slice_in_dim(query_rows, row_start, block_rows, 0)
        scores = block_scores(
            query_piece, key_rows, block_mask(segment_ids, row_start, seq_start, block_rows)
        )
        peak = jnp.max(scores, axis=-1, keepdims=True)
        raised = jnp.exp(scores - peak)
        denominator = jnp.sum(raised, axis=-1, keepdims=True)
        weights = (raised / denominator).astype(jnp.bfloat16)
        attended = jnp.einsum(
            "hqk,khd->qhd", weights, value_rows, preferred_element_type=jnp.float32
        )
        return (attended.astype(jnp.bfloat16), (peak + jnp.log(denominator))[..., 0])

    attended, logsum = lax.map(one_block, jnp.arange(block_count))
    return (attended.reshape(token_count, heads_here * head_size), logsum)


def attend_backward(query_rows, key_rows, value_rows, mixed_grad, logsum, segment_ids):
    token_count, heads_here, head_size = query_rows.shape
    block_rows = min(512, SEQ)
    block_count = token_count // block_rows
    score_scale = HEAD_DIM ** (-0.5)

    def one_block(carry, pieces):
        key_grad, value_grad = carry
        index_block, logsum_piece = pieces
        row_start = index_block * block_rows
        seq_start = row_start // SEQ * SEQ
        query_piece = lax.dynamic_slice_in_dim(query_rows, row_start, block_rows, 0)
        grad_piece = lax.dynamic_slice_in_dim(mixed_grad, row_start, block_rows, 0)
        scores = block_scores(
            query_piece, key_rows, block_mask(segment_ids, row_start, seq_start, block_rows)
        )
        weights = jnp.exp(scores - logsum_piece[..., None])
        weight_grad = jnp.einsum(
            "qhd,khd->hqk", grad_piece, value_rows, preferred_element_type=jnp.float32
        )
        row_dots = jnp.sum(weights * weight_grad, axis=-1, keepdims=True)
        score_grad = (weights * (weight_grad - row_dots)).astype(jnp.bfloat16)
        query_grad = (
            jnp.einsum("hqk,khd->qhd", score_grad, key_rows, preferred_element_type=jnp.float32)
            * score_scale
        )
        key_add = (
            jnp.einsum("hqk,qhd->khd", score_grad, query_piece, preferred_element_type=jnp.float32)
            * score_scale
        )
        value_add = jnp.einsum(
            "hqk,qhd->khd",
            weights.astype(jnp.bfloat16),
            grad_piece,
            preferred_element_type=jnp.float32,
        )
        key_grad = key_grad + key_add
        value_grad = value_grad + value_add
        return ((key_grad, value_grad), query_grad)

    zeros_grad = jnp.zeros((token_count, heads_here, head_size), jnp.float32)
    (key_grad, value_grad), query_grad = lax.scan(
        one_block, (zeros_grad, zeros_grad), (jnp.arange(block_count), logsum)
    )
    return (query_grad.reshape(token_count, heads_here, head_size), key_grad, value_grad)


def local(
    inputs,
    query_weight,
    key_weight,
    value_weight,
    out_weight,
    gate_weight,
    up_weight,
    down_weight,
    first_gain,
    second_gain,
    segment_ids,
    positions,
    out_grad,
):
    col_index = lax.axis_index("col")
    feat_here = inputs.shape[1]
    width = feat_here * lax.axis_size("col")
    token_count = inputs.shape[0]
    heads_here = query_weight.shape[1] // HEAD_DIM
    gathered = (
        lax.all_gather(query_weight, "row", axis=0, tiled=True),
        lax.all_gather(key_weight, "row", axis=0, tiled=True),
        lax.all_gather(value_weight, "row", axis=0, tiled=True),
        lax.all_gather(out_weight, "row", axis=0, tiled=True),
        lax.all_gather(gate_weight, "row", axis=0, tiled=True),
        lax.all_gather(up_weight, "row", axis=0, tiled=True),
        lax.all_gather(down_weight, "row", axis=0, tiled=True),
        lax.all_gather(first_gain, "row", axis=0, tiled=True),
        lax.all_gather(second_gain, "row", axis=0, tiled=True),
    )
    (
        query_full,
        key_full,
        value_full,
        out_full,
        gate_full,
        up_full,
        down_full,
        gain_one,
        gain_two,
    ) = gathered
    gain_one = gain_one.astype(jnp.float32)
    gain_two = gain_two.astype(jnp.float32)
    gain_one_block = lax.dynamic_slice_in_dim(gain_one, col_index * feat_here, feat_here, 0)
    gain_two_block = lax.dynamic_slice_in_dim(gain_two, col_index * feat_here, feat_here, 0)
    input_rows = lax.all_gather(inputs, "col", axis=1, tiled=True).astype(jnp.float32)
    scale_one = lax.rsqrt(jnp.mean(input_rows * input_rows, axis=1, keepdims=True) + eps)
    unit_one = input_rows * scale_one
    normed_one = (unit_one * gain_one).astype(jnp.bfloat16)
    cosine, sine = rope_tables(positions, HEAD_DIM)
    query_pre = jnp.dot(normed_one, query_full, preferred_element_type=jnp.float32).reshape(
        token_count, heads_here, HEAD_DIM
    )
    key_pre = jnp.dot(normed_one, key_full, preferred_element_type=jnp.float32).reshape(
        token_count, heads_here, HEAD_DIM
    )
    query_rows = rotate(query_pre, cosine, sine).astype(jnp.bfloat16)
    key_rows = rotate(key_pre, cosine, sine).astype(jnp.bfloat16)
    value_rows = (
        jnp.dot(normed_one, value_full, preferred_element_type=jnp.float32)
        .astype(jnp.bfloat16)
        .reshape(token_count, heads_here, HEAD_DIM)
    )
    mixed, logsum = attend_forward(query_rows, key_rows, value_rows, segment_ids)
    input_block = inputs.astype(jnp.float32)
    attention_part = contract_last(mixed, out_full)
    attention_block = lax.psum_scatter(attention_part, "col", scatter_dimension=1, tiled=True)
    middle_block = input_block + attention_block
    middle_rows = lax.all_gather(middle_block, "col", axis=1, tiled=True)
    scale_two = lax.rsqrt(jnp.mean(middle_rows * middle_rows, axis=1, keepdims=True) + eps)
    unit_two = middle_rows * scale_two
    normed_two = (unit_two * gain_two).astype(jnp.bfloat16)
    gate_rows = jnp.dot(normed_two, gate_full, preferred_element_type=jnp.float32)
    up_rows = jnp.dot(normed_two, up_full, preferred_element_type=jnp.float32)
    sigmoid_gate = jax.nn.sigmoid(gate_rows)
    silu_gate = gate_rows * sigmoid_gate
    hidden = (silu_gate * up_rows).astype(jnp.bfloat16)
    feed_part = contract_last(hidden, down_full)
    feed_block = lax.psum_scatter(
        feed_part.astype(jnp.bfloat16), "col", scatter_dimension=1, tiled=True
    ).astype(jnp.float32)
    block_out = (middle_block + feed_block).astype(jnp.bfloat16)
    grad_rows = lax.all_gather(out_grad, "col", axis=1, tiled=True)
    hidden_grad = jnp.dot(grad_rows, down_full, preferred_element_type=jnp.float32)
    down_weight_grad = contract_first(grad_rows, hidden)
    gate_grad = (
        hidden_grad * up_rows * sigmoid_gate * (1.0 + gate_rows * (1.0 - sigmoid_gate))
    ).astype(jnp.bfloat16)
    up_grad = (hidden_grad * silu_gate).astype(jnp.bfloat16)
    gate_weight_grad = contract_first(normed_two, gate_grad)
    up_weight_grad = contract_first(normed_two, up_grad)
    normed_two_grad = contract_last(gate_grad, gate_full) + contract_last(up_grad, up_full)
    gain_two_part = jnp.sum(normed_two_grad * unit_two, axis=0)
    token_two_part = jnp.sum(normed_two_grad * gain_two * unit_two, axis=1)
    token_two, gain_two_grad = lax.psum((token_two_part, gain_two_part), "col")
    normed_two_block = lax.psum_scatter(
        normed_two_grad.astype(jnp.bfloat16), "col", scatter_dimension=1, tiled=True
    ).astype(jnp.float32)
    unit_two_block = lax.dynamic_slice_in_dim(unit_two, col_index * feat_here, feat_here, 1)
    middle_grad = out_grad.astype(jnp.float32) + scale_two * (
        normed_two_block * gain_two_block - unit_two_block * (token_two[:, None] / width)
    )
    middle_rows_grad = lax.all_gather(middle_grad.astype(jnp.bfloat16), "col", axis=1, tiled=True)
    mixed_grad = jnp.dot(middle_rows_grad, out_full, preferred_element_type=jnp.float32).astype(
        jnp.bfloat16
    )
    out_weight_grad = contract_first(middle_rows_grad, mixed)
    query_grad, key_grad, value_grad = attend_backward(
        query_rows,
        key_rows,
        value_rows,
        mixed_grad.reshape(token_count, heads_here, HEAD_DIM),
        logsum,
        segment_ids,
    )
    query_grad = (
        unrotate(query_grad, cosine, sine)
        .astype(jnp.bfloat16)
        .reshape(token_count, heads_here * HEAD_DIM)
    )
    key_grad = (
        unrotate(key_grad, cosine, sine)
        .astype(jnp.bfloat16)
        .reshape(token_count, heads_here * HEAD_DIM)
    )
    value_grad = value_grad.astype(jnp.bfloat16).reshape(token_count, heads_here * HEAD_DIM)
    query_weight_grad = contract_first(normed_one, query_grad)
    key_weight_grad = contract_first(normed_one, key_grad)
    value_weight_grad = contract_first(normed_one, value_grad)
    normed_one_grad = (
        contract_last(query_grad, query_full)
        + contract_last(key_grad, key_full)
        + contract_last(value_grad, value_full)
    )
    gain_one_part = jnp.sum(normed_one_grad * unit_one, axis=0)
    token_one_part = jnp.sum(normed_one_grad * gain_one * unit_one, axis=1)
    token_one, gain_one_grad = lax.psum((token_one_part, gain_one_part), "col")
    normed_one_block = lax.psum_scatter(
        normed_one_grad.astype(jnp.bfloat16), "col", scatter_dimension=1, tiled=True
    ).astype(jnp.float32)
    unit_one_block = lax.dynamic_slice_in_dim(unit_one, col_index * feat_here, feat_here, 1)
    input_grad = (
        middle_grad
        + scale_one
        * (normed_one_block * gain_one_block - unit_one_block * (token_one[:, None] / width))
    ).astype(jnp.bfloat16)
    summed = (
        lax.psum_scatter(
            query_weight_grad.astype(jnp.bfloat16), "row", scatter_dimension=0, tiled=True
        ).astype(jnp.float32),
        lax.psum_scatter(
            key_weight_grad.astype(jnp.bfloat16), "row", scatter_dimension=0, tiled=True
        ).astype(jnp.float32),
        lax.psum_scatter(
            value_weight_grad.astype(jnp.bfloat16), "row", scatter_dimension=0, tiled=True
        ).astype(jnp.float32),
        lax.psum_scatter(
            out_weight_grad.astype(jnp.bfloat16), "row", scatter_dimension=0, tiled=True
        ).astype(jnp.float32),
        lax.psum_scatter(
            gate_weight_grad.astype(jnp.bfloat16), "row", scatter_dimension=0, tiled=True
        ).astype(jnp.float32),
        lax.psum_scatter(
            up_weight_grad.astype(jnp.bfloat16), "row", scatter_dimension=0, tiled=True
        ).astype(jnp.float32),
        lax.psum_scatter(
            down_weight_grad.astype(jnp.bfloat16), "row", scatter_dimension=0, tiled=True
        ).astype(jnp.float32),
        lax.psum_scatter(
            gain_one_grad.astype(jnp.bfloat16), "row", scatter_dimension=0, tiled=True
        ).astype(jnp.float32),
        lax.psum_scatter(
            gain_two_grad.astype(jnp.bfloat16), "row", scatter_dimension=0, tiled=True
        ).astype(jnp.float32),
    )
    return (block_out, input_grad) + tuple(summed)


def solution(mesh):
    return jax.shard_map(
        local,
        mesh=mesh,
        in_specs=(
            P("row", "col"),
            P("row", "col"),
            P("row", "col"),
            P("row", "col"),
            P("row", "col"),
            P("row", "col"),
            P("row", "col"),
            P("row", "col"),
            P("row"),
            P("row"),
            P("row"),
            P("row"),
            P("row", "col"),
        ),
        out_specs=(
            P("row", "col"),
            P("row", "col"),
            P("row", "col"),
            P("row", "col"),
            P("row", "col"),
            P("row", "col"),
            P("row", "col"),
            P("row", "col"),
            P("row", "col"),
            P("row"),
            P("row"),
        ),
        check_vma=False,
    )
```

profile of v0, /device:TPU:0, one launch (start us, length us, event | category | flops | bytes accessed | tf_op | source)
XLA Modules:
  0.0 1178.5 jit_solution(17229201245399395030)
XLA Ops:
  12.0 13.5 %all-gather = bf16[4,1,512]{2,1,0:T(2,128)(2,1)S(1)} all-gather(bf16[1,1,512]{2,1,0:T(2,128)(2,1)S(1)} %reshape.296), channel_id=1, replica_groups=mesh['row'=4,'col'=8] {'row'}, dimensions={0}, use_global_device_ids=true | all-gather | bytes 5120 | tf_op jit(solution)/shard_map/all_gather | solution.py:180
  26.1 23.9 %all-gather.14.cloned.1.call-done = bf16[1024,2048]{1,0:T(8,128)(2,1)} async-done(((bf16[1024,256]{1,0:T(8,128)(2,1)}), bf16[1024,2048]{1,0:T(8,128)(2,1)}) %all-gather.14.cloned.1.call-update) | async-done | bytes 4194320 | tf_op jit(solution)/shard_map/all_gather | solution.py:198
  56.6 23.0 %all-gather.18.cloned.1.call-done = bf16[2048,256]{1,0:T(8,128)(2,1)} async-done(((bf16[512,256]{1,0:T(8,128)(2,1)}), bf16[2048,256]{1,0:T(8,128)(2,1)}) %all-gather.18.cloned.1.call-update) | async-done | bytes 1048592 | tf_op jit(solution)/shard_map/all_gather | solution.py:174
  83.4 25.3 %all-gather.16.cloned.1.call-done = bf16[2048,256]{1,0:T(8,128)(2,1)} async-done(((bf16[512,256]{1,0:T(8,128)(2,1)}), bf16[2048,256]{1,0:T(8,128)(2,1)}) %all-gather.16.cloned.1.call-update) | async-done | bytes 1048592 | tf_op jit(solution)/shard_map/all_gather | solution.py:173
  112.8 24.7 %all-gather.20.cloned.1.call-done = bf16[2048,256]{1,0:T(8,128)(2,1)} async-done(((bf16[512,256]{1,0:T(8,128)(2,1)}), bf16[2048,256]{1,0:T(8,128)(2,1)}) %all-gather.20.cloned.1.call-update) | async-done | bytes 1048592 | tf_op jit(solution)/shard_map/all_gather | solution.py:175
  137.5 3.8 convolution_convert_fusion.8
  141.3 18.4 %while.31 = (s32[]{:T(128)}, bf16[2,512,4,64]{1,3,2,0:T(8,128)(2,1)S(1)}, f32[2,4,512]{2,1,0:T(4,128)S(1)}, s32[2]{0:T(128)S(1)}, s32[1024]{0:T(1024)S(1)}, /*in...) while((s32[]{:T(128)}, ...), condition=%wide.region_4.5_spmd, body=%wide.region_1.4_spmd.sunk | while | flops 563740160 | bytes 28924288 | solution.py:101
  160.3 6.1 all-gather.22.cloned.1.call-done
  166.4 5.8 fusion.41
  172.3 70.9 %reduce-scatter.12.cloned.1.call-done = f32[1024,256]{1,0:T(8,128)} async-done(((f32[1024,2048]{1,0:T(8,128)}), f32[1024,256]{1,0:T(8,128)}) %reduce-scatter.12.cloned.1.call-update) | async-done | bytes 1048592 | tf_op jit(solution)/shard_map/reduce_scatter | solution.py:219
  248.4 12.1 %all-gather.1 = bf16[4,1,512]{2,1,0:T(2,128)(2,1)S(1)} all-gather(bf16[1,1,512]{2,1,0:T(2,128)(2,1)S(1)} %reshape.298), channel_id=1, replica_groups=mesh['row'=4,'col'=8] {'row'}, dimensions={0}, use_global_device_ids=true | all-gather | bytes 5120 | tf_op jit(solution)/shard_map/all_gather | solution.py:181
  260.5 41.1 %all-gather.24.cloned.1.call-done = f32[1024,2048]{1,0:T(8,128)} async-done(((f32[1024,256]{1,0:T(8,128)}), f32[1024,2048]{1,0:T(8,128)}) %all-gather.24.cloned.1.call-update) | async-done | bytes 8388624 | tf_op jit(solution)/shard_map/all_gather | solution.py:221
  301.6 4.1 multiply_reduce_fusion.5
  307.3 6.1 multiply_convert_fusion.1
  313.4 70.6 %all-gather.28.cloned.1.call-done = bf16[2048,1024]{1,0:T(8,128)(2,1)} async-done(((bf16[512,1024]{1,0:T(8,128)(2,1)}), bf16[2048,1024]{1,0:T(8,128)(2,1)}) %all-gather.28.cloned.1.call-update) | async-done | bytes 4194320 | tf_op jit(solution)/shard_map/all_gather | solution.py:178
  384.0 9.9 fusion.43
  393.9 71.1 %all-gather.26.cloned.1.call-done = bf16[2048,1024]{1,0:T(8,128)(2,1)} async-done(((bf16[512,1024]{1,0:T(8,128)(2,1)}), bf16[2048,1024]{1,0:T(8,128)(2,1)}) %all-gather.26.cloned.1.call-update) | async-done | bytes 4194320 | tf_op jit(solution)/shard_map/all_gather | solution.py:177
  465.0 10.0 fusion.42
  475.0 70.8 %all-gather.30.cloned.1.call-done = bf16[2048,1024]{1,0:T(8,128)(2,1)} async-done(((bf16[512,1024]{1,0:T(8,128)(2,1)}), bf16[2048,1024]{1,0:T(8,128)(2,1)}) %all-gather.30.cloned.1.call-update) | async-done | bytes 4194320 | tf_op jit(solution)/shard_map/all_gather | solution.py:179
  545.8 38.0 %all-gather.32.cloned.1.call-done = bf16[1024,2048]{1,0:T(8,128)(2,1)} async-done(((bf16[1024,256]{1,0:T(8,128)(2,1)}), bf16[1024,2048]{1,0:T(8,128)(2,1)}) %all-gather.32.cloned.1.call-update) | async-done | bytes 4194320 | tf_op jit(solution)/shard_map/all_gather | solution.py:235
  583.9 14.0 %multiply_convert_fusion.3 = (bf16[1024,1024]{1,0:T(8,128)(2,1)}, bf16[1024,1024]{1,0:T(8,128)(2,1)S(1)}, bf16[1024,1024]{1,0:T(8,128)(2,1)}) fusion(f32[1024,1024]{1,0:T(8,128)} %fusion.42, f32[1024,1024]{1,0:T(8,128)} %fusion.43, bf16[1024,2048]{1,0:T(8,128)(2,1)} %all-gather.32.cloned.1.call-done, bf16[2048,1024]{1,0:T(8,128)(2,1)} %all-gather.30.cloned.1.call-done), kind=kOutput, calls=%fused_computation.59 | convolution fusion | flops 4310695936 | bytes 23068672 | tf_op jit(solution)/shard_map/dot_general | solution.py:236
  597.8 7.0 fusion.44
  604.9 11.7 multiply_reduce_fusion.1
  616.8 13.1 %psum.28 = f32[1024]{0:T(1024)S(1)} all-reduce(f32[1024]{0:T(1024)S(1)} %get-tuple-element.329), channel_id=1, replica_groups=mesh['row'=4,'col'=8] {'col'}, use_global_device_ids=true, to_apply=%region_10.11 | all-reduce | flops 1024 | bytes 8192 | tf_op jit(solution)/shard_map/psum | solution.py:247
  629.9 38.2 %reduce-scatter.16.cloned.1.call-done = bf16[1024,256]{1,0:T(8,128)(2,1)} async-done(((bf16[1024,2048]{1,0:T(8,128)(2,1)}), bf16[1024,256]{1,0:T(8,128)(2,1)}) %reduce-scatter.16.cloned.1.call-update) | async-done | bytes 524304 | tf_op jit(solution)/shard_map/reduce_scatter | solution.py:248
  670.7 9.4 convolution_convert_fusion.2
  680.6 9.4 convert_bitcast_fusion
  690.0 9.7 convolution_convert_fusion
  699.9 9.6 convolution_convert_fusion.1
  709.6 4.5 convolution_convert_fusion.3
  714.3 4.6 convolution_convert_fusion.7
  718.9 54.1 %while.32 = (s32[]{:T(128)}, f32[1024,4,64]{0,2,1:T(8,128)S(1)}, f32[1024,4,64]{0,2,1:T(8,128)}, f32[2,512,4,64]{1,0,3,2:T(2,128)}, s32[2]{0:T(128)S(1)}, /*inde...) while((s32[]{:T(128)}, f32[1024,4,64]{0,2,1:T(8,128)S(1)}, ...), condition=%wide.region_13.14_spmd.clone, body=%wide.region_11.13_spmd.clone.sunk | while | flops 1376648704 | bytes 82917864 | solution.py:146
  725.7 4.5 multiply_reduce_fusion.7
  735.5 10.4 dynamic_update_slice.29
  752.7 4.5 multiply_reduce_fusion.7
  762.6 10.4 dynamic_update_slice.29
  774.3 4.6 convolution_convert_fusion.4
  786.0 4.6 convolution_convert_fusion.5
  793.4 8.5 multiply_reduce_fusion.2
  805.8 36.1 %reduce-scatter.32.cloned.1.call-done = bf16[512,1024]{0,1:T(8,128)(2,1)} async-done(((bf16[2048,1024]{0,1:T(8,128)(2,1)}), bf16[512,1024]{0,1:T(8,128)(2,1)}) %reduce-scatter.32.cloned.1.call-update) | async-done | bytes 1048592 | tf_op jit(solution)/shard_map/reduce_scatter | solution.py:318
  844.5 76.9 %reduce-scatter.30.cloned.1.call-done = bf16[512,1024]{1,0:T(8,128)(2,1)} async-done(((bf16[2048,1024]{1,0:T(8,128)(2,1)}), bf16[512,1024]{1,0:T(8,128)(2,1)}) %reduce-scatter.30.cloned.1.call-update) | async-done | bytes 1048592 | tf_op jit(solution)/shard_map/reduce_scatter | solution.py:315
  924.1 76.8 %reduce-scatter.28.cloned.1.call-done = bf16[512,1024]{1,0:T(8,128)(2,1)} async-done(((bf16[2048,1024]{1,0:T(8,128)(2,1)}), bf16[512,1024]{1,0:T(8,128)(2,1)}) %reduce-scatter.28.cloned.1.call-update) | async-done | bytes 1048592 | tf_op jit(solution)/shard_map/reduce_scatter | solution.py:312
  1003.7 25.2 %all-reduce.2 = (f32[1024]{0:T(1024)S(1)}, bf16[2048]{0:T(1024)(128)(2,1)S(1)}, bf16[2048]{0:T(1024)(128)(2,1)S(1)}) all-reduce(f32[1024]{0:T(1024)S(1)} %get-tuple-element.331, f32[2048]{0:T(1024)S(1)} %get-tuple-element.330, f32[2048]{0:T(1024)S(1)} %copy-done.28), channel_id=1, replica_groups=mesh['row'=4,'col'=8] {'col'}, use_global_device_ids=true, to_apply=%region_16.17 | all-reduce | flops 5120 | bytes 32768 | tf_op jit(solution)/shard_map/psum | solution.py:289
  1028.9 11.4 all-reduce.3
  1043.4 15.5 %reduce-scatter.24.cloned.1.call-done = bf16[512,256]{1,0:T(8,128)(2,1)} async-done(((bf16[2048,256]{1,0:T(8,128)(2,1)}), bf16[512,256]{1,0:T(8,128)(2,1)}) %reduce-scatter.24.cloned.1.call-update) | async-done | bytes 262160 | tf_op jit(solution)/shard_map/reduce_scatter | solution.py:306
  1060.7 26.2 %reduce-scatter.20.cloned.1.call-done = bf16[512,256]{1,0:T(8,128)(2,1)} async-done(((bf16[2048,256]{1,0:T(8,128)(2,1)}), bf16[512,256]{1,0:T(8,128)(2,1)}) %reduce-scatter.20.cloned.1.call-update) | async-done | bytes 262160 | tf_op jit(solution)/shard_map/reduce_scatter | solution.py:300
  1088.7 26.5 %reduce-scatter.22.cloned.1.call-done = bf16[512,256]{1,0:T(8,128)(2,1)} async-done(((bf16[2048,256]{1,0:T(8,128)(2,1)}), bf16[512,256]{1,0:T(8,128)(2,1)}) %reduce-scatter.22.cloned.1.call-update) | async-done | bytes 262160 | tf_op jit(solution)/shard_map/reduce_scatter | solution.py:303
  1116.9 51.6 %reduce-scatter.18.cloned.1.call-done = bf16[1024,256]{1,0:T(8,128)(2,1)} async-done(((bf16[1024,2048]{1,0:T(8,128)(2,1)}), bf16[1024,256]{1,0:T(8,128)(2,1)}) %reduce-scatter.18.cloned.1.call-update) | async-done | bytes 524304 | tf_op jit(solution)/shard_map/reduce_scatter | solution.py:290
  (211 shorter events, 103.5 us)
Async XLA Ops:
  7.2 42.9 %all-gather.14.cloned.1.call-start = ((), (), s32[]{:S(2)}) async-start(), calls=%async_computation.11 | async-start | bytes 4718592 | tf_op jit(solution)/shard_map/all_gather | solution.py:198
  7.9 71.7 %all-gather.18.cloned.1.call-start = ((), (), s32[]{:S(2)}) async-start(), calls=%async_computation.13 | async-start | bytes 1310720 | tf_op jit(solution)/shard_map/all_gather | solution.py:174
  8.7 100.0 %all-gather.16.cloned.1.call-start = ((), (), s32[]{:S(2)}) async-start(), calls=%async_computation.12 | async-start | bytes 1310720 | tf_op jit(solution)/shard_map/all_gather | solution.py:173
  9.4 128.1 %all-gather.20.cloned.1.call-start = ((), (), s32[]{:S(2)}) async-start(), calls=%async_computation.14 | async-start | bytes 1310720 | tf_op jit(solution)/shard_map/all_gather | solution.py:175
  10.0 156.4 %all-gather.22.cloned.1.call-start = ((), (), s32[]{:S(2)}) async-start(), calls=%async_computation.15 | async-start | bytes 1310720 | tf_op jit(solution)/shard_map/all_gather | solution.py:176
  10.6 232.6 %reduce-scatter.12.cloned.1.call-start = ((), (), s32[]{:S(2)}) async-start(), calls=%async_computation.16 | async-start | bytes 9437184 | tf_op jit(solution)/shard_map/reduce_scatter | solution.py:219
  25.6 31.0 %copy-start.18 = (f32[4,1,512]{2,1,0:T(1,128)}, f32[4,1,512]{2,1,0:T(1,128)S(1)}, u32[]{:S(2)}) copy-start(f32[4,1,512]{2,1,0:T(1,128)S(1)} %convert_element_type.209) | copy-start | bytes 24580
  26.1 86.3 %copy-start.8 = (f32[1024,32]{0,1:T(8,128)}, f32[1024,32]{0,1:T(8,128)S(1)}, u32[]{:S(2)}) copy-start(f32[1024,32]{0,1:T(8,128)S(1)} %get-tuple-element.399) | copy-start | bytes 393220
  26.1 86.3 %copy-start.10 = (f32[1024,32]{0,1:T(8,128)}, f32[1024,32]{0,1:T(8,128)S(1)}, u32[]{:S(2)}) copy-start(f32[1024,32]{0,1:T(8,128)S(1)} %get-tuple-element.400) | copy-start | bytes 393220
  50.1 3.4 copy-start
  112.8 28.5 %copy-start.17 = (s32[1024]{0:T(1024)S(1)}, s32[1024]{0:T(1024)}, u32[]{:S(2)}) copy-start(s32[1024]{0:T(1024)} %param.27) | copy-start | bytes 12292
  172.2 71.0 %copy-start.6 = (bf16[1024,256]{1,0:T(8,128)(2,1)S(1)}, bf16[1024,256]{1,0:T(8,128)(2,1)}, u32[]{:S(2)}) copy-start(bf16[1024,256]{1,0:T(8,128)(2,1)} %param.17) | copy-start | bytes 1572868
  172.2 76.1 %copy-start.29 = (bf16[512]{0:T(512)(128)(2,1)S(1)}, bf16[512]{0:T(512)(128)(2,1)}, u32[]{:S(2)}) copy-start(bf16[512]{0:T(512)(128)(2,1)} %param.26) | copy-start | bytes 3076
  172.2 129.3 %all-gather.24.cloned.1.call-start = ((), (), s32[]{:S(2)}) async-start(), calls=%async_computation.17 | async-start | bytes 9437184 | tf_op jit(solution)/shard_map/all_gather | solution.py:221
  245.5 138.5 %all-gather.28.cloned.1.call-start = ((), (), s32[]{:S(2)}) async-start(), calls=%async_computation.19 | async-start | bytes 5242880 | tf_op jit(solution)/shard_map/all_gather | solution.py:178
  246.2 218.8 %all-gather.26.cloned.1.call-start = ((), (), s32[]{:S(2)}) async-start(), calls=%async_computation.18 | async-start | bytes 5242880 | tf_op jit(solution)/shard_map/all_gather | solution.py:177
  247.0 298.8 %all-gather.30.cloned.1.call-start = ((), (), s32[]{:S(2)}) async-start(), calls=%async_computation.20 | async-start | bytes 5242880 | tf_op jit(solution)/shard_map/all_gather | solution.py:179
  247.6 336.3 %all-gather.32.cloned.1.call-start = ((), (), s32[]{:S(2)}) async-start(), calls=%async_computation.22 | async-start | bytes 4718592 | tf_op jit(solution)/shard_map/all_gather | solution.py:235
  248.3 419.8 %reduce-scatter.16.cloned.1.call-start = ((), (), s32[]{:S(2)}) async-start(), calls=%async_computation.23 | async-start | bytes 4718592 | tf_op jit(solution)/shard_map/reduce_scatter | solution.py:248
  301.6 5.8 copy-start.1
  305.7 362.4 %copy-start.22 = (f32[1024]{0:T(1024)}, f32[1024]{0:T(1024)S(1)}, u32[]{:S(2)}) copy-start(f32[1024]{0:T(1024)S(1)} %add_rsqrt_fusion) | copy-start | bytes 12292
  583.9 14.0 %copy-start.31 = (bf16[2048,1024]{1,0:T(8,128)(2,1)S(1)}, bf16[2048,1024]{1,0:T(8,128)(2,1)}, u32[]{:S(2)}) copy-start(bf16[2048,1024]{1,0:T(8,128)(2,1)} %all-gather.26.cloned.1.call-done) | copy-start | bytes 12582916
  597.8 7.0 copy-start.33
  597.8 7.0 copy-start.30
  616.6 51.5 %copy-start.3 = (bf16[1024,256]{1,0:T(8,128)(2,1)S(1)}, bf16[1024,256]{1,0:T(8,128)(2,1)}, u32[]{:S(2)}) copy-start(bf16[1024,256]{1,0:T(8,128)(2,1)} %param.29) | copy-start | bytes 1572868
  616.7 92.9 %all-gather.34.cloned.1.call-start = ((), (), s32[]{:S(2)}) async-start(), calls=%async_computation.24 | async-start | bytes 4718592 | tf_op jit(solution)/shard_map/all_gather | solution.py:255
  616.8 63.3 %copy-start.26 = (f32[256]{0:T(256)}, f32[256]{0:T(256)S(1)}, u32[]{:S(2)}) copy-start(f32[256]{0:T(256)S(1)} %dynamic_slice.62) | copy-start | bytes 3076
  629.9 50.2 %copy-start.24 = (f32[1024]{0:T(1024)}, f32[1024]{0:T(1024)S(1)}, u32[]{:S(2)}) copy-start(f32[1024]{0:T(1024)S(1)} %broadcast_multiply_fusion.2) | copy-start | bytes 12292
  670.7 133.1 %reduce-scatter.14.cloned.1.call-start = ((), (), s32[]{:S(2)}) async-start(), calls=%async_computation.21 | async-start | bytes 4718592 | tf_op jit(solution)/shard_map/reduce_scatter | solution.py:231
  680.1 161.7 %reduce-scatter.32.cloned.1.call-start = ((), (), s32[]{:S(2)}) async-start(), calls=%async_computation.32 | async-start | bytes 5242880 | tf_op jit(solution)/shard_map/reduce_scatter | solution.py:318
  690.0 231.3 %reduce-scatter.30.cloned.1.call-start = ((), (), s32[]{:S(2)}) async-start(), calls=%async_computation.31 | async-start | bytes 5242880 | tf_op jit(solution)/shard_map/reduce_scatter | solution.py:315
  699.8 301.1 %reduce-scatter.28.cloned.1.call-start = ((), (), s32[]{:S(2)}) async-start(), calls=%async_computation.30 | async-start | bytes 5242880 | tf_op jit(solution)/shard_map/reduce_scatter | solution.py:312
  709.5 332.2 %reduce-scatter.26.cloned.1.call-start = ((), (), s32[]{:S(2)}) async-start(), calls=%async_computation.29 | async-start | bytes 1310720 | tf_op jit(solution)/shard_map/reduce_scatter | solution.py:309
  714.1 344.8 %reduce-scatter.24.cloned.1.call-start = ((), (), s32[]{:S(2)}) async-start(), calls=%async_computation.28 | async-start | bytes 1310720 | tf_op jit(solution)/shard_map/reduce_scatter | solution.py:306
  725.7 4.6 copy-start.16
  752.7 4.6 copy-start.16
  774.3 7.0 copy-start.9
  774.3 7.0 copy-start.11
  778.9 308.0 %reduce-scatter.20.cloned.1.call-start = ((), (), s32[]{:S(2)}) async-start(), calls=%async_computation.26 | async-start | bytes 1310720 | tf_op jit(solution)/shard_map/reduce_scatter | solution.py:300
  785.9 329.2 %reduce-scatter.22.cloned.1.call-start = ((), (), s32[]{:S(2)}) async-start(), calls=%async_computation.27 | async-start | bytes 1310720 | tf_op jit(solution)/shard_map/reduce_scatter | solution.py:303
  786.0 4.7 copy-start.12
  790.6 377.9 %reduce-scatter.18.cloned.1.call-start = ((), (), s32[]{:S(2)}) async-start(), calls=%async_computation.25 | async-start | bytes 4718592 | tf_op jit(solution)/shard_map/reduce_scatter | solution.py:290
  805.8 197.9 %copy-start.28 = (f32[2048]{0:T(1024)S(1)}, f32[2048]{0:T(1024)}, u32[]{:S(2)}) copy-start(f32[2048]{0:T(1024)} %get-tuple-element.328) | copy-start | bytes 24580
  844.4 324.0 %copy-start.4 = (bf16[1024,256]{1,0:T(8,128)(2,1)S(1)}, bf16[1024,256]{1,0:T(8,128)(2,1)}, u32[]{:S(2)}) copy-start(bf16[1024,256]{1,0:T(8,128)(2,1)} %param.29) | copy-start | bytes 1572868
  844.4 324.0 %copy-start.7 = (bf16[1024,256]{1,0:T(8,128)(2,1)S(1)}, bf16[1024,256]{1,0:T(8,128)(2,1)}, u32[]{:S(2)}) copy-start(bf16[1024,256]{1,0:T(8,128)(2,1)} %reduce-scatter.16.cloned.1.call-done) | copy-start | bytes 1572868
  844.4 324.0 %copy-start.23 = (f32[1024]{0:T(1024)S(1)}, f32[1024]{0:T(1024)}, u32[]{:S(2)}) copy-start(f32[1024]{0:T(1024)} %copy-done.22) | copy-start | bytes 12292
  844.5 324.0 %copy-start.25 = (f32[1024]{0:T(1024)S(1)}, f32[1024]{0:T(1024)}, u32[]{:S(2)}) copy-start(f32[1024]{0:T(1024)} %copy-done.24) | copy-start | bytes 12292
  844.5 324.0 %copy-start.27 = (f32[256]{0:T(256)S(1)}, f32[256]{0:T(256)}, u32[]{:S(2)}) copy-start(f32[256]{0:T(256)} %copy-done.26) | copy-start | bytes 3076
  (10 other events, 16.1 us)
Sparse Core Ops, SparseCore 0:
  9.9 40.1 all-gather.13
  51.6 27.9 all-gather.17
  81.2 27.4 all-gather.15
  110.0 27.4 all-gather.19
  138.9 27.4 all-gather.21
  172.3 70.7 reduce-scatter.11
  245.6 55.9 all-gather.23
  303.2 80.7 all-gather.27
  385.7 79.2 all-gather.25
  466.5 79.2 all-gather.29
  547.9 35.9 all-gather.31
  616.8 51.3 reduce-scatter.15
  670.8 37.4 all-gather.33
  711.5 51.3 reduce-scatter.13
  765.1 76.7 reduce-scatter.31
  844.0 77.2 reduce-scatter.29
  923.6 77.2 reduce-scatter.27
  1003.0 27.6 reduce-scatter.25
  1033.1 25.7 reduce-scatter.23
  1061.1 25.7 reduce-scatter.19
  1089.3 25.7 reduce-scatter.21
  1118.5 49.9 reduce-scatter.17
where the time goes:
time: 1190 us; the launch traced here: 1180 us
  waiting for transfers between devices  819 us (69%)
  matrix products  173 us (15%)
  blocking collectives  75.4 us (6%)
  other arithmetic  54.9 us (5%)
  local copies, waits for them, and re-layouts  35.6 us (3%)
  between operations  15.7 us (1%)
    reduce_scatter x1, waiting for transfers between devices, local(): lax.psum_scatter(up_weight_grad.astype(jnp.bfloat16), 'row', scatter_dime...  76.9 us
    reduce_scatter x1, waiting for transfers between devices, local(): lax.psum_scatter(gate_weight_grad.astype(jnp.bfloat16), 'row', scatter_di...  76.8 us
    all_gather x1, waiting for transfers between devices, local(): lax.all_gather(gate_weight, 'row', axis=0, tiled=True)  71.1 us
    reduce_scatter x1, waiting for transfers between devices, local(): lax.psum_scatter(attention_part, 'col', scatter_dimension=1, tiled=True)  70.9 us
    all_gather x1, waiting for transfers between devices, local(): lax.all_gather(down_weight, 'row', axis=0, tiled=True)  70.8 us
    all_gather x1, waiting for transfers between devices, local(): lax.all_gather(up_weight, 'row', axis=0, tiled=True)  70.6 us
    reduce_scatter x1, waiting for transfers between devices, local(): lax.psum_scatter(normed_one_grad.astype(jnp.bfloat16), 'col', scatter_dim...  51.6 us
    dot_general x7, matrix products, contract_last(): lax.dot_general(left, right, (((1,), (1,)), ((), ())), preferred_element_...  45.1 us
  transfers between devices with their start and end apart: 22, of which 19 were waited for; matrix products, arithmetic and copies ran while one was open for 18% of the time, Pallas kernels for 0%

commit v1 on v0

--- a/solution.py
+++ b/solution.py
@@ -1,3 +1,4 @@
+import functools
 import math
 import jax
 import jax.numpy as jnp
@@ -8,6 +9,23 @@
 SEQ = 1024
 eps = 1e-05
 rope_base = 130000.0
+
+
+def serve_masks(work_x, link_axis):
+    dev_count = lax.axis_size(link_axis)
+    outer = work_x
+    steps_seen = [outer]
+    val = sorted(((tick, (tick + 1) % dev_count) for tick in range(dev_count)))
+    for k0 in range(1, dev_count):
+        outer = lax.ppermute(outer, link_axis, val)
+        steps_seen.insert(0, outer)
+    last = jnp.concatenate(steps_seen, 1)
+    shaped = lax.axis_index(link_axis)
+    e_now = shaped + 1
+    return jnp.roll(last, e_now * work_x.shape[1], 1)
+
+
+_open_tasks = functools.partial(serve_masks, link_axis="col")
 
 
 def rope_tables(positions, head_size):
@@ -218,7 +236,7 @@
     attention_part = contract_last(mixed, out_full)
     attention_block = lax.psum_scatter(attention_part, "col", scatter_dimension=1, tiled=True)
     middle_block = input_block + attention_block
-    middle_rows = lax.all_gather(middle_block, "col", axis=1, tiled=True)
+    middle_rows = _open_tasks(middle_block)
     scale_two = lax.rsqrt(jnp.mean(middle_rows * middle_rows, axis=1, keepdims=True) + eps)
     unit_two = middle_rows * scale_two
     normed_two = (unit_two * gain_two).astype(jnp.bfloat16)

time: 1190 us -> 1140 us (0.958)
  waiting for transfers between devices: 819 us -> 730 us
  matrix products: 173 us -> 193 us
  local copies, waits for them, and re-layouts: 35.6 us -> 54.9 us
    ppermute x0 -> x7, waiting for transfers between devices: none -> 83.5 us  [serve_masks(): outer = lax.ppermute(outer, link_axis, val)]
    all_gather x1, waiting for transfers between devices: 70.8 us -> 0.02 us  [local(): lax.all_gather(down_weight, 'row', axis=0, tiled=True)]
    reduce_scatter x1, waiting for transfers between devices: 76.8 us -> 14.1 us  [local(): lax.psum_scatter(gate_weight_grad.astype(jnp.bfloat16), 'row', scatter_di...]
    all_gather x1 -> x0, waiting for transfers between devices: 41.1 us -> none  [local(): middle_rows = lax.all_gather(middle_block, 'col', axis=1, tiled=True)]
    reduce_scatter x1, waiting for transfers between devices: 36.1 us -> 76.8 us  [local(): lax.psum_scatter(down_weight_grad.astype(jnp.bfloat16), 'row', scatter_di...]
    reduce_scatter x1, waiting for transfers between devices: 0.01 us -> 26.3 us  [local(): lax.psum_scatter(out_weight_grad.astype(jnp.bfloat16), 'row', scatter_dim...]
    reduce_scatter x1, waiting for transfers between devices: 26.2 us -> 0.01 us  [local(): lax.psum_scatter(query_weight_grad.astype(jnp.bfloat16), 'row', scatter_d...]
    all_gather x1, waiting for transfers between devices: 70.6 us -> 45.8 us  [local(): lax.all_gather(up_weight, 'row', axis=0, tiled=True)]
  transfers between devices with their start and end apart: 22 -> 28, of which waited for: 19 -> 23; matrix products, arithmetic and copies ran while one was open for 18% -> 22% of each run, Pallas kernels for 0% -> 0%
where the time goes in v1:
time: 1140 us; the launch traced here: 1130 us
  waiting for transfers between devices  730 us (64%)
  matrix products  193 us (17%)
  blocking collectives  75.7 us (7%)
  other arithmetic  56.1 us (5%)
  local copies, waits for them, and re-layouts  54.9 us (5%)
  between operations  15.9 us (1%)
    ppermute x7, waiting for transfers between devices, serve_masks(): outer = lax.ppermute(outer, link_axis, val)  83.5 us
    reduce_scatter x1, waiting for transfers between devices, local(): lax.psum_scatter(down_weight_grad.astype(jnp.bfloat16), 'row', scatter_di...  76.8 us
    reduce_scatter x1, waiting for transfers between devices, local(): lax.psum_scatter(up_weight_grad.astype(jnp.bfloat16), 'row', scatter_dime...  76.6 us
    all_gather x1, waiting for transfers between devices, local(): lax.all_gather(gate_weight, 'row', axis=0, tiled=True)  70.9 us
    reduce_scatter x1, waiting for transfers between devices, local(): lax.psum_scatter(attention_part, 'col', scatter_dimension=1, tiled=True)  68.6 us
    reduce_scatter x1, waiting for transfers between devices, local(): lax.psum_scatter(normed_one_grad.astype(jnp.bfloat16), 'col', scatter_dim...  51.6 us
    dot_general x7, matrix products, contract_last(): lax.dot_general(left, right, (((1,), (1,)), ((), ())), preferred_element_...  47.8 us
    all_gather x1, waiting for transfers between devices, local(): lax.all_gather(up_weight, 'row', axis=0, tiled=True)  45.8 us
  transfers between devices with their start and end apart: 28, of which 23 were waited for; matrix products, arithmetic and copies ran while one was open for 22% of the time, Pallas kernels for 0%

profile of v1, /device:TPU:0, one launch (start us, length us, event | category | flops | bytes accessed | tf_op | source)
XLA Modules:
  0.0 1130.2 jit_solution(5721128677385392574)
XLA Ops:
  11.3 13.5 %all-gather = bf16[4,1,512]{2,1,0:T(2,128)(2,1)S(1)} all-gather(bf16[1,1,512]{2,1,0:T(2,128)(2,1)S(1)} %reshape.296), channel_id=1, replica_groups=mesh['row'=4,'col'=8] {'row'}, dimensions={0}, use_global_device_ids=true | all-gather | bytes 5120 | tf_op jit(solution)/shard_map/all_gather | solution.py:198
  26.1 23.9 %all-gather.13.cloned.1.call-done = bf16[1024,2048]{1,0:T(8,128)(2,1)} async-done(((bf16[1024,256]{1,0:T(8,128)(2,1)}), bf16[1024,2048]{1,0:T(8,128)(2,1)}) %all-gather.13.cloned.1.call-update) | async-done | bytes 4194320 | tf_op jit(solution)/shard_map/all_gather | solution.py:216
  56.5 23.1 %all-gather.17.cloned.1.call-done = bf16[2048,256]{1,0:T(8,128)(2,1)} async-done(((bf16[512,256]{1,0:T(8,128)(2,1)}), bf16[2048,256]{1,0:T(8,128)(2,1)}) %all-gather.17.cloned.1.call-update) | async-done | bytes 1048592 | tf_op jit(solution)/shard_map/all_gather | solution.py:192
  83.4 25.3 %all-gather.15.cloned.1.call-done = bf16[2048,256]{1,0:T(8,128)(2,1)} async-done(((bf16[512,256]{1,0:T(8,128)(2,1)}), bf16[2048,256]{1,0:T(8,128)(2,1)}) %all-gather.15.cloned.1.call-update) | async-done | bytes 1048592 | tf_op jit(solution)/shard_map/all_gather | solution.py:191
  112.8 24.7 %all-gather.19.cloned.1.call-done = bf16[2048,256]{1,0:T(8,128)(2,1)} async-done(((bf16[512,256]{1,0:T(8,128)(2,1)}), bf16[2048,256]{1,0:T(8,128)(2,1)}) %all-gather.19.cloned.1.call-update) | async-done | bytes 1048592 | tf_op jit(solution)/shard_map/all_gather | solution.py:193
  141.3 18.1 %while.31 = (s32[]{:T(128)}, bf16[2,512,4,64]{1,3,2,0:T(8,128)(2,1)S(1)}, f32[2,4,512]{2,1,0:T(4,128)S(1)}, s32[2]{0:T(128)S(1)}, s32[1024]{0:T(1024)S(1)}, /*in...) while((s32[]{:T(128)}, ...), condition=%wide.region_4.5_spmd, body=%wide.region_1.4_spmd.sunk | while | flops 563740160 | bytes 28924288 | solution.py:119
  160.1 6.3 all-gather.21.cloned.1.call-done
  166.4 5.8 fusion.41
  174.5 68.6 %reduce-scatter.12.cloned.1.call-done = f32[1024,256]{1,0:T(8,128)} async-done(((f32[1024,2048]{1,0:T(8,128)}), f32[1024,256]{1,0:T(8,128)}) %reduce-scatter.12.cloned.1.call-update) | async-done | bytes 1048592 | tf_op jit(solution)/shard_map/reduce_scatter | solution.py:237
  244.6 15.1 %collective-permute-done = f32[1024,256]{1,0:T(8,128)S(1)} collective-permute-done((f32[1024,256]{1,0:T(8,128)S(1)}, f32[1024,256]{1,0:T(8,128)S(1)}, u32[]{:S(2)}, u32[]{:S(2)}) %collective-permute-start) | collective-permute-done | bytes 1048608 | tf_op jit(solution)/shard_map/ppermute | solution.py:20
  260.7 15.1 %collective-permute-done.1 = f32[1024,256]{1,0:T(8,128)S(1)} collective-permute-done((f32[1024,256]{1,0:T(8,128)S(1)}, f32[1024,256]{1,0:T(8,128)S(1)}, u32[]{:S(2)}, u32[]{:S(2)}) %collective-permute-start.1) | collective-permute-done | bytes 1048608 | tf_op jit(solution)/shard_map/ppermute | solution.py:20
  276.8 15.1 %collective-permute-done.2 = f32[1024,256]{1,0:T(8,128)S(1)} collective-permute-done((f32[1024,256]{1,0:T(8,128)S(1)}, f32[1024,256]{1,0:T(8,128)S(1)}, u32[]{:S(2)}, u32[]{:S(2)}) %collective-permute-start.2) | collective-permute-done | bytes 1048608 | tf_op jit(solution)/shard_map/ppermute | solution.py:20
  292.9 15.1 %collective-permute-done.3 = f32[1024,256]{1,0:T(8,128)S(1)} collective-permute-done((f32[1024,256]{1,0:T(8,128)S(1)}, f32[1024,256]{1,0:T(8,128)S(1)}, u32[]{:S(2)}, u32[]{:S(2)}) %collective-permute-start.3) | collective-permute-done | bytes 1048608 | tf_op jit(solution)/shard_map/ppermute | solution.py:20
  309.0 15.2 %collective-permute-done.4 = f32[1024,256]{1,0:T(8,128)} collective-permute-done((f32[1024,256]{1,0:T(8,128)S(1)}, f32[1024,256]{1,0:T(8,128)}, u32[]{:S(2)}, u32[]{:S(2)}) %collective-permute-start.4) | collective-permute-done | bytes 1048608 | tf_op jit(solution)/shard_map/ppermute | solution.py:20
  324.3 11.9 %all-gather.1 = bf16[4,1,512]{2,1,0:T(2,128)(2,1)S(1)} all-gather(bf16[1,1,512]{2,1,0:T(2,128)(2,1)S(1)} %reshape.298), channel_id=1, replica_groups=mesh['row'=4,'col'=8] {'row'}, dimensions={0}, use_global_device_ids=true | all-gather | bytes 5120 | tf_op jit(solution)/shard_map/all_gather | solution.py:199
  336.2 7.8 collective-permute-done.5
  344.2 28.6 %all-gather.29.cloned.1.call-done = bf16[1024,2048]{1,0:T(8,128)(2,1)} async-done(((bf16[1024,256]{1,0:T(8,128)(2,1)}), bf16[1024,2048]{1,0:T(8,128)(2,1)}) %all-gather.29.cloned.1.call-update) | async-done | bytes 4194320 | tf_op jit(solution)/shard_map/all_gather | solution.py:253
  372.8 9.9 fusion.43
  392.9 5.8 copy-done.2
  399.4 9.2 multiply_convert_fusion.1
  408.6 45.8 %all-gather.25.cloned.1.call-done = bf16[2048,1024]{1,0:T(8,128)(2,1)} async-done(((bf16[512,1024]{1,0:T(8,128)(2,1)}), bf16[2048,1024]{1,0:T(8,128)(2,1)}) %all-gather.25.cloned.1.call-update) | async-done | bytes 4194320 | tf_op jit(solution)/shard_map/all_gather | solution.py:196
  454.3 9.9 fusion.42
  464.3 70.9 %all-gather.23.cloned.1.call-done = bf16[2048,1024]{1,0:T(8,128)(2,1)} async-done(((bf16[512,1024]{1,0:T(8,128)(2,1)}), bf16[2048,1024]{1,0:T(8,128)(2,1)}) %all-gather.23.cloned.1.call-update) | async-done | bytes 4194320 | tf_op jit(solution)/shard_map/all_gather | solution.py:195
  535.2 14.6 %multiply_convert_fusion.3 = (bf16[1024,1024]{1,0:T(8,128)(2,1)}, bf16[1024,1024]{1,0:T(8,128)(2,1)S(1)}, bf16[1024,1024]{1,0:T(8,128)(2,1)}) fusion(f32[1024,1024]{1,0:T(8,128)} %fusion.43, f32[1024,1024]{1,0:T(8,128)} %fusion.42, bf16[1024,2048]{1,0:T(8,128)(2,1)} %get-tuple-element.375, bf16[2048,1024]{1,0:T(8,128)(2,1)} %all-gather.23.cloned.1.call-done), kind=kOutput, calls=%fused_computation.60 | convolution fusion | flops 4310695936 | bytes 23068672 | tf_op jit(solution)/shard_map/dot_general | solution.py:243
  549.8 6.7 fusion.44
  556.6 13.3 %multiply_reduce_fusion.1 = (f32[2048]{0:T(1024)}, f32[1024]{0:T(1024)S(1)}, bf16[1024,2048]{1,0:T(8,128)(2,1)}) fusion(f32[1024,2048]{1,0:T(8,128)S(1)} %copy-done.5, f32[2048]{0:T(1024)S(1)} %bitcast.141, f32[1024,2048]{1,0:T(8,128)} %fusion.44, bf16[1024,1024]{1,0:T(8,128)(2,1)} %get-tuple-element.383, bf16[2048,1024]{1,0:T(8,128)(2,1)} %all-gather.25.cloned.1.call-done), kind=kOutput, calls=%fused_computation.50 | convolution fusion | flops 4309644288 | bytes 27283456 | tf_op jit(solution)/shard_map/dot_general | solution.py:71
  570.1 13.6 %psum.28 = f32[1024]{0:T(1024)S(1)} all-reduce(f32[1024]{0:T(1024)S(1)} %get-tuple-element.329), channel_id=1, replica_groups=mesh['row'=4,'col'=8] {'col'}, use_global_device_ids=true, to_apply=%region_10.11 | all-reduce | flops 1024 | bytes 8192 | tf_op jit(solution)/shard_map/psum | solution.py:265
  583.7 36.2 %reduce-scatter.16.cloned.1.call-done = bf16[1024,256]{1,0:T(8,128)(2,1)} async-done(((bf16[1024,2048]{1,0:T(8,128)(2,1)}), bf16[1024,256]{1,0:T(8,128)(2,1)}) %reduce-scatter.16.cloned.1.call-update) | async-done | bytes 524304 | tf_op jit(solution)/shard_map/reduce_scatter | solution.py:266
  622.5 9.4 convolution_convert_fusion.2
  632.2 9.4 convolution_convert_fusion.1
  641.6 9.5 convolution_convert_fusion
  651.3 9.5 convert_bitcast_fusion
  665.5 75.5 %while.32 = (s32[]{:T(128)}, f32[1024,4,64]{0,2,1:T(8,128)S(1)}, f32[1024,4,64]{0,2,1:T(8,128)}, f32[2,512,4,64]{1,0,3,2:T(2,128)}, s32[2]{0:T(128)S(1)}, /*inde...) while((s32[]{:T(128)}, f32[1024,4,64]{0,2,1:T(8,128)S(1)}, ...), condition=%wide.region_13.14_spmd.clone, body=%wide.region_11.13_spmd.clone.sunk | while | flops 1376648704 | bytes 126958168 | solution.py:164
  672.4 6.2 multiply_reduce_fusion.7
  693.5 10.4 dynamic_update_slice.29
  710.4 5.8 multiply_reduce_fusion.7
  723.5 5.0 fusion.130
  730.6 10.4 dynamic_update_slice.29
  767.3 8.5 multiply_reduce_fusion.2
  779.7 14.1 %reduce-scatter.28.cloned.1.call-done = bf16[512,1024]{1,0:T(8,128)(2,1)} async-done(((bf16[2048,1024]{1,0:T(8,128)(2,1)}), bf16[512,1024]{1,0:T(8,128)(2,1)}) %reduce-scatter.28.cloned.1.call-update) | async-done | bytes 1048592 | tf_op jit(solution)/shard_map/reduce_scatter | solution.py:330
  796.6 76.6 %reduce-scatter.30.cloned.1.call-done = bf16[512,1024]{1,0:T(8,128)(2,1)} async-done(((bf16[2048,1024]{1,0:T(8,128)(2,1)}), bf16[512,1024]{1,0:T(8,128)(2,1)}) %reduce-scatter.30.cloned.1.call-update) | async-done | bytes 1048592 | tf_op jit(solution)/shard_map/reduce_scatter | solution.py:333
  876.0 76.8 %reduce-scatter.32.cloned.1.call-done = bf16[512,1024]{0,1:T(8,128)(2,1)} async-done(((bf16[2048,1024]{0,1:T(8,128)(2,1)}), bf16[512,1024]{0,1:T(8,128)(2,1)}) %reduce-scatter.32.cloned.1.call-update) | async-done | bytes 1048592 | tf_op jit(solution)/shard_map/reduce_scatter | solution.py:336
  955.4 25.2 %all-reduce.2 = (f32[1024]{0:T(1024)S(1)}, bf16[2048]{0:T(1024)(128)(2,1)S(1)}, bf16[2048]{0:T(1024)(128)(2,1)S(1)}) all-reduce(f32[1024]{0:T(1024)S(1)} %get-tuple-element.331, f32[2048]{0:T(1024)S(1)} %get-tuple-element.330, f32[2048]{0:T(1024)S(1)} %copy-done.41), channel_id=1, replica_groups=mesh['row'=4,'col'=8] {'col'}, use_global_device_ids=true, to_apply=%region_16.17 | all-reduce | flops 5120 | bytes 32768 | tf_op jit(solution)/shard_map/psum | solution.py:307
  980.6 11.4 %all-reduce.3 = (bf16[2048]{0:T(1024)(128)(2,1)S(1)}, bf16[2048]{0:T(1024)(128)(2,1)S(1)}) all-reduce(bf16[2048]{0:T(1024)(128)(2,1)S(1)} %get-tuple-element.371, bf16[2048]{0:T(1024)(128)(2,1)S(1)} %get-tuple-element.372), channel_id=13, replica_groups=mesh['row'=4,'col'=8] {'row'}, use_global_device_ids=true, to_apply=%region_26.27.clone | all-reduce | flops 4096 | bytes 16384
  995.1 15.6 %reduce-scatter.22.cloned.1.call-done = bf16[512,256]{1,0:T(8,128)(2,1)} async-done(((bf16[2048,256]{1,0:T(8,128)(2,1)}), bf16[512,256]{1,0:T(8,128)(2,1)}) %reduce-scatter.22.cloned.1.call-update) | async-done | bytes 262160 | tf_op jit(solution)/shard_map/reduce_scatter | solution.py:321
  1012.5 26.3 %reduce-scatter.24.cloned.1.call-done = bf16[512,256]{1,0:T(8,128)(2,1)} async-done(((bf16[2048,256]{1,0:T(8,128)(2,1)}), bf16[512,256]{1,0:T(8,128)(2,1)}) %reduce-scatter.24.cloned.1.call-update) | async-done | bytes 262160 | tf_op jit(solution)/shard_map/reduce_scatter | solution.py:324
  1040.6 26.3 %reduce-scatter.26.cloned.1.call-done = bf16[512,256]{1,0:T(8,128)(2,1)} async-done(((bf16[2048,256]{1,0:T(8,128)(2,1)}), bf16[512,256]{1,0:T(8,128)(2,1)}) %reduce-scatter.26.cloned.1.call-update) | async-done | bytes 262160 | tf_op jit(solution)/shard_map/reduce_scatter | solution.py:327
  1068.7 51.6 %reduce-scatter.18.cloned.1.call-done = bf16[1024,256]{1,0:T(8,128)(2,1)} async-done(((bf16[1024,2048]{1,0:T(8,128)(2,1)}), bf16[1024,256]{1,0:T(8,128)(2,1)}) %reduce-scatter.18.cloned.1.call-update) | async-done | bytes 524304 | tf_op jit(solution)/shard_map/reduce_scatter | solution.py:308
  (276 shorter events, 151.2 us)
Async XLA Ops:
  7.2 42.9 %all-gather.13.cloned.1.call-start = ((), (), s32[]{:S(2)}) async-start(), calls=%async_computation.11 | async-start | bytes 4718592 | tf_op jit(solution)/shard_map/all_gather | solution.py:216
  7.9 71.7 %all-gather.17.cloned.1.call-start = ((), (), s32[]{:S(2)}) async-start(), calls=%async_computation.13 | async-start | bytes 1310720 | tf_op jit(solution)/shard_map/all_gather | solution.py:192
  8.7 100.0 %all-gather.15.cloned.1.call-start = ((), (), s32[]{:S(2)}) async-start(), calls=%async_computation.12 | async-start | bytes 1310720 | tf_op jit(solution)/shard_map/all_gather | solution.py:191
  9.4 128.1 %all-gather.19.cloned.1.call-start = ((), (), s32[]{:S(2)}) async-start(), calls=%async_computation.14 | async-start | bytes 1310720 | tf_op jit(solution)/shard_map/all_gather | solution.py:193
  10.0 156.4 %all-gather.21.cloned.1.call-start = ((), (), s32[]{:S(2)}) async-start(), calls=%async_computation.15 | async-start | bytes 1310720 | tf_op jit(solution)/shard_map/all_gather | solution.py:194
  10.6 232.6 %reduce-scatter.12.cloned.1.call-start = ((), (), s32[]{:S(2)}) async-start(), calls=%async_computation.16 | async-start | bytes 9437184 | tf_op jit(solution)/shard_map/reduce_scatter | solution.py:237
  24.9 31.6 %copy-start.31 = (f32[4,1,512]{2,1,0:T(1,128)}, f32[4,1,512]{2,1,0:T(1,128)S(1)}, u32[]{:S(2)}) copy-start(f32[4,1,512]{2,1,0:T(1,128)S(1)} %convert_element_type.209) | copy-start | bytes 24580
  26.1 86.3 %copy-start.22 = (f32[1024,32]{0,1:T(8,128)}, f32[1024,32]{0,1:T(8,128)S(1)}, u32[]{:S(2)}) copy-start(f32[1024,32]{0,1:T(8,128)S(1)} %get-tuple-element.399) | copy-start | bytes 393220
  26.1 86.3 %copy-start.24 = (f32[1024,32]{0,1:T(8,128)}, f32[1024,32]{0,1:T(8,128)S(1)}, u32[]{:S(2)}) copy-start(f32[1024,32]{0,1:T(8,128)S(1)} %get-tuple-element.400) | copy-start | bytes 393220
  112.8 28.5 %copy-start.30 = (s32[1024]{0:T(1024)S(1)}, s32[1024]{0:T(1024)}, u32[]{:S(2)}) copy-start(s32[1024]{0:T(1024)} %param.27) | copy-start | bytes 12292
  172.2 70.9 %copy-start.20 = (bf16[1024,256]{1,0:T(8,128)(2,1)S(1)}, bf16[1024,256]{1,0:T(8,128)(2,1)}, u32[]{:S(2)}) copy-start(bf16[1024,256]{1,0:T(8,128)(2,1)} %param.17) | copy-start | bytes 1572868
  172.2 152.0 %copy-start.42 = (bf16[512]{0:T(512)(128)(2,1)S(1)}, bf16[512]{0:T(512)(128)(2,1)}, u32[]{:S(2)}) copy-start(bf16[512]{0:T(512)(128)(2,1)} %param.26) | copy-start | bytes 3076
  172.3 172.0 %all-gather.27.cloned.1.call-start = ((), (), s32[]{:S(2)}) async-start(), calls=%async_computation.19 | async-start | bytes 5242880 | tf_op jit(solution)/shard_map/all_gather | solution.py:197
  173.0 199.8 %all-gather.29.cloned.1.call-start = ((), (), s32[]{:S(2)}) async-start(), calls=%async_computation.21 | async-start | bytes 4718592 | tf_op jit(solution)/shard_map/all_gather | solution.py:253
  173.8 280.6 %all-gather.25.cloned.1.call-start = ((), (), s32[]{:S(2)}) async-start(), calls=%async_computation.18 | async-start | bytes 5242880 | tf_op jit(solution)/shard_map/all_gather | solution.py:196
  174.5 360.7 %all-gather.23.cloned.1.call-start = ((), (), s32[]{:S(2)}) async-start(), calls=%async_computation.17 | async-start | bytes 5242880 | tf_op jit(solution)/shard_map/all_gather | solution.py:195
  244.5 148.3 %copy-start.3 = (f32[1024,256]{1,0:T(8,128)}, f32[1024,256]{1,0:T(8,128)S(1)}, u32[]{:S(2)}) copy-start(f32[1024,256]{1,0:T(8,128)S(1)} %convert_add_fusion) | copy-start | bytes 3145732
  244.5 15.2 %collective-permute-start = (f32[1024,256]{1,0:T(8,128)S(1)}, f32[1024,256]{1,0:T(8,128)S(1)}, u32[]{:S(2)}, u32[]{:S(2)}) collective-permute-start(f32[1024,256]{1,0:T(8,128)S(1)} %convert_add_fusion), channel_id=1, source_target_pairs={{0,1},{1,2},{2,3},{3,4},{4,5},{5,6},{6,7},{7,0},{8,9},{9,10},{10,1... | collective-permute-start | bytes 3145736 | tf_op jit(solution)/shard_map/ppermute | solution.py:20
  260.7 15.1 %collective-permute-start.1 = (f32[1024,256]{1,0:T(8,128)S(1)}, f32[1024,256]{1,0:T(8,128)S(1)}, u32[]{:S(2)}, u32[]{:S(2)}) collective-permute-start(f32[1024,256]{1,0:T(8,128)S(1)} %collective-permute-done), channel_id=1, source_target_pairs={{0,1},{1,2},{2,3},{3,4},{4,5},{5,6},{6,7},{7,0},{8,9},{9,10},{10,1... | collective-permute-start | bytes 3145736 | tf_op jit(solution)/shard_map/ppermute | solution.py:20
  276.8 15.1 %collective-permute-start.2 = (f32[1024,256]{1,0:T(8,128)S(1)}, f32[1024,256]{1,0:T(8,128)S(1)}, u32[]{:S(2)}, u32[]{:S(2)}) collective-permute-start(f32[1024,256]{1,0:T(8,128)S(1)} %collective-permute-done.1), channel_id=1, source_target_pairs={{0,1},{1,2},{2,3},{3,4},{4,5},{5,6},{6,7},{7,0},{8,9},{9,10},{10,1... | collective-permute-start | bytes 3145736 | tf_op jit(solution)/shard_map/ppermute | solution.py:20
  292.9 15.1 %collective-permute-start.3 = (f32[1024,256]{1,0:T(8,128)S(1)}, f32[1024,256]{1,0:T(8,128)S(1)}, u32[]{:S(2)}, u32[]{:S(2)}) collective-permute-start(f32[1024,256]{1,0:T(8,128)S(1)} %collective-permute-done.2), channel_id=1, source_target_pairs={{0,1},{1,2},{2,3},{3,4},{4,5},{5,6},{6,7},{7,0},{8,9},{9,10},{10,1... | collective-permute-start | bytes 3145736 | tf_op jit(solution)/shard_map/ppermute | solution.py:20
  309.0 15.2 %collective-permute-start.4 = (f32[1024,256]{1,0:T(8,128)S(1)}, f32[1024,256]{1,0:T(8,128)}, u32[]{:S(2)}, u32[]{:S(2)}) collective-permute-start(f32[1024,256]{1,0:T(8,128)S(1)} %collective-permute-done.3), channel_id=1, source_target_pairs={{0,1},{1,2},{2,3},{3,4},{4,5},{5,6},{6,7},{7,0},{8,9},{9,10},{10,1... | collective-permute-start | bytes 3145736 | tf_op jit(solution)/shard_map/ppermute | solution.py:20
  324.2 19.8 %collective-permute-start.5 = (f32[1024,256]{1,0:T(8,128)}, f32[1024,256]{1,0:T(8,128)}, u32[]{:S(2)}, u32[]{:S(2)}) collective-permute-start(f32[1024,256]{1,0:T(8,128)} %collective-permute-done.4), channel_id=1, source_target_pairs={{0,1},{1,2},{2,3},{3,4},{4,5},{5,6},{6,7},{7,0},{8,9},{9,10},{10,1... | collective-permute-start | bytes 3145736 | tf_op jit(solution)/shard_map/ppermute | solution.py:20
  324.2 295.7 %reduce-scatter.16.cloned.1.call-start = ((), (), s32[]{:S(2)}) async-start(), calls=%async_computation.22 | async-start | bytes 4718592 | tf_op jit(solution)/shard_map/reduce_scatter | solution.py:266
  344.0 38.7 %collective-permute-start.6 = (f32[1024,256]{1,0:T(8,128)}, f32[1024,256]{1,0:T(8,128)}, u32[]{:S(2)}, u32[]{:S(2)}) collective-permute-start(f32[1024,256]{1,0:T(8,128)} %collective-permute-done.5), channel_id=1, source_target_pairs={{0,1},{1,2},{2,3},{3,4},{4,5},{5,6},{6,7},{7,0},{8,9},{9,10},{10,1... | collective-permute-start | bytes 3145736 | tf_op jit(solution)/shard_map/ppermute | solution.py:20
  399.3 220.6 %copy-start.35 = (f32[1024]{0:T(1024)}, f32[1024]{0:T(1024)S(1)}, u32[]{:S(2)}) copy-start(f32[1024]{0:T(1024)S(1)} %add_rsqrt_fusion) | copy-start | bytes 12292
  535.2 14.6 %copy-start.43 = (bf16[2048,1024]{1,0:T(8,128)(2,1)S(1)}, bf16[2048,1024]{1,0:T(8,128)(2,1)}, u32[]{:S(2)}) copy-start(bf16[2048,1024]{1,0:T(8,128)(2,1)} %all-gather.23.cloned.1.call-done) | copy-start | bytes 12582916
  569.9 50.0 %copy-start.6 = (bf16[1024,256]{1,0:T(8,128)(2,1)S(1)}, bf16[1024,256]{1,0:T(8,128)(2,1)}, u32[]{:S(2)}) copy-start(bf16[1024,256]{1,0:T(8,128)(2,1)} %param.29) | copy-start | bytes 1572868
  569.9 91.0 %all-gather.31.cloned.1.call-start = ((), (), s32[]{:S(2)}) async-start(), calls=%async_computation.23 | async-start | bytes 4718592 | tf_op jit(solution)/shard_map/all_gather | solution.py:273
  570.0 61.9 %copy-start.39 = (f32[256]{0:T(256)}, f32[256]{0:T(256)S(1)}, u32[]{:S(2)}) copy-start(f32[256]{0:T(256)S(1)} %dynamic_slice.67) | copy-start | bytes 3076
  583.7 48.2 %copy-start.37 = (f32[1024]{0:T(1024)}, f32[1024]{0:T(1024)S(1)}, u32[]{:S(2)}) copy-start(f32[1024]{0:T(1024)S(1)} %broadcast_multiply_fusion.1) | copy-start | bytes 12292
  622.4 155.3 %reduce-scatter.14.cloned.1.call-start = ((), (), s32[]{:S(2)}) async-start(), calls=%async_computation.20 | async-start | bytes 4718592 | tf_op jit(solution)/shard_map/reduce_scatter | solution.py:249
  632.0 161.9 %reduce-scatter.28.cloned.1.call-start = ((), (), s32[]{:S(2)}) async-start(), calls=%async_computation.29 | async-start | bytes 5242880 | tf_op jit(solution)/shard_map/reduce_scatter | solution.py:330
  641.6 231.6 %reduce-scatter.30.cloned.1.call-start = ((), (), s32[]{:S(2)}) async-start(), calls=%async_computation.30 | async-start | bytes 5242880 | tf_op jit(solution)/shard_map/reduce_scatter | solution.py:333
  651.2 301.6 %reduce-scatter.32.cloned.1.call-start = ((), (), s32[]{:S(2)}) async-start(), calls=%async_computation.31 | async-start | bytes 5242880 | tf_op jit(solution)/shard_map/reduce_scatter | solution.py:336
  660.8 332.5 %reduce-scatter.20.cloned.1.call-start = ((), (), s32[]{:S(2)}) async-start(), calls=%async_computation.25 | async-start | bytes 1310720 | tf_op jit(solution)/shard_map/reduce_scatter | solution.py:318
  665.5 77.6 %copy-start.23 = (f32[1024,32]{0,1:T(8,128)S(1)}, f32[1024,32]{0,1:T(8,128)}, u32[]{:S(2)}) copy-start(f32[1024,32]{0,1:T(8,128)} %copy-done.22) | copy-start | bytes 393220
  665.5 77.6 %copy-start.25 = (f32[1024,32]{0,1:T(8,128)S(1)}, f32[1024,32]{0,1:T(8,128)}, u32[]{:S(2)}) copy-start(f32[1024,32]{0,1:T(8,128)} %copy-done.24) | copy-start | bytes 393220
  747.7 263.0 %reduce-scatter.22.cloned.1.call-start = ((), (), s32[]{:S(2)}) async-start(), calls=%async_computation.26 | async-start | bytes 1310720 | tf_op jit(solution)/shard_map/reduce_scatter | solution.py:321
  752.6 286.3 %reduce-scatter.24.cloned.1.call-start = ((), (), s32[]{:S(2)}) async-start(), calls=%async_computation.27 | async-start | bytes 1310720 | tf_op jit(solution)/shard_map/reduce_scatter | solution.py:324
  758.5 308.4 %reduce-scatter.26.cloned.1.call-start = ((), (), s32[]{:S(2)}) async-start(), calls=%async_computation.28 | async-start | bytes 1310720 | tf_op jit(solution)/shard_map/reduce_scatter | solution.py:327
  763.2 357.1 %reduce-scatter.18.cloned.1.call-start = ((), (), s32[]{:S(2)}) async-start(), calls=%async_computation.24 | async-start | bytes 4718592 | tf_op jit(solution)/shard_map/reduce_scatter | solution.py:308
  779.7 175.7 %copy-start.41 = (f32[2048]{0:T(1024)S(1)}, f32[2048]{0:T(1024)}, u32[]{:S(2)}) copy-start(f32[2048]{0:T(1024)} %get-tuple-element.328) | copy-start | bytes 24580
  796.6 323.7 %copy-start.7 = (bf16[1024,256]{1,0:T(8,128)(2,1)S(1)}, bf16[1024,256]{1,0:T(8,128)(2,1)}, u32[]{:S(2)}) copy-start(bf16[1024,256]{1,0:T(8,128)(2,1)} %param.29) | copy-start | bytes 1572868
  796.6 323.7 %copy-start.21 = (bf16[1024,256]{1,0:T(8,128)(2,1)S(1)}, bf16[1024,256]{1,0:T(8,128)(2,1)}, u32[]{:S(2)}) copy-start(bf16[1024,256]{1,0:T(8,128)(2,1)} %reduce-scatter.16.cloned.1.call-done) | copy-start | bytes 1572868
  796.6 323.7 %copy-start.36 = (f32[1024]{0:T(1024)S(1)}, f32[1024]{0:T(1024)}, u32[]{:S(2)}) copy-start(f32[1024]{0:T(1024)} %copy-done.35) | copy-start | bytes 12292
  796.6 323.7 %copy-start.38 = (f32[1024]{0:T(1024)S(1)}, f32[1024]{0:T(1024)}, u32[]{:S(2)}) copy-start(f32[1024]{0:T(1024)} %copy-done.37) | copy-start | bytes 12292
  796.6 323.7 %copy-start.40 = (f32[256]{0:T(256)S(1)}, f32[256]{0:T(256)}, u32[]{:S(2)}) copy-start(f32[256]{0:T(256)} %copy-done.39) | copy-start | bytes 3076
  (34 other events, 124.1 us)
Sparse Core Ops, SparseCore 0:
  9.9 40.1 all-gather.12
  51.6 27.9 all-gather.16
  81.2 27.4 all-gather.14
  110.0 27.4 all-gather.18
  138.9 27.4 all-gather.20
  172.4 70.7 reduce-scatter.11
  244.8 80.7 all-gather.26
  327.6 45.1 all-gather.28
  374.5 79.8 all-gather.24
  455.8 79.2 all-gather.22
  570.0 49.8 reduce-scatter.15
  622.6 37.4 all-gather.30
  663.4 51.3 reduce-scatter.13
  717.0 76.7 reduce-scatter.27
  796.0 77.2 reduce-scatter.29
  875.5 77.2 reduce-scatter.31
  954.9 27.6 reduce-scatter.19
  984.9 25.8 reduce-scatter.21
  1013.0 25.7 reduce-scatter.23
  1041.1 25.7 reduce-scatter.25
  1070.3 49.9 reduce-scatter.17
